TPU v7x, 256 devices: a whole 4x4x8 slice. The times are simulated.
256 devices in a mesh: ctx: 32 (over y, x, core), head: 8 (over z).
Axes of the slice: x: 4, y: 4, z: 8, core: 2. Of those that a mesh axis runs over, the one named last changes fastest.
Arguments:
- query_key: bfloat16 [16384, 1024], P('ctx', 'head'), may hold values from -6 to 6
- values: bfloat16 [16384, 4096], P('ctx', 'head'), may hold values from -6 to 6
- out_grad: bfloat16 [16384, 4096], P('ctx', 'head'), may hold values from -6 to 6
- out_weight: bfloat16 [4096, 4096], P('head'), may hold values from -0.09375 to 0.09375
- doc_lengths: int32 [128], replicated, may hold values from 1 to 2048, 16384 in all
Outputs:
- qk_grad: bfloat16 [16384, 1024], P('ctx', 'head')
- value_grad: bfloat16 [16384, 4096], P('ctx', 'head')
- proj_grad: float32 [4096, 4096], P('head', 'ctx')
Inputs may be any that keep to these rules, and one draw needn't show every extreme that they name: `doc_lengths`: the documents fill all 16384 positions in order; the longest has exactly 2048 tokens.
All inputs are finite; a program needn't handle non-finite values.
Results may differ from a plain program's by a relative error of at most 0.0068.
Values may be sent and summed in bfloat16 or wider, within the bound.
No kernel may reach another device: no remote copies, remote signals or barrier semaphores. Data moves between devices by JAX's collectives and lax.ppermute only.
A program may use at most 128 MiB of HBM per device.

v0:
```python
import math

import jax
import jax.numpy as jnp
from jax import lax
from jax.sharding import PartitionSpec as P

HEAD = 128
QK = 16


quad_scale = 0.25 / math.sqrt(2.0)
highest = lax.Precision.HIGHEST


def prefix(x, axis, combine, identity, reverse):
    count, here = (lax.axis_size(axis), lax.axis_index(axis))
    everything = jax.tree.map(lambda part: lax.all_gather(part, axis), x)
    start = jax.tree.map(
        lambda part, zero: jnp.broadcast_to(jnp.asarray(zero, part.dtype), part.shape), x, identity
    )

    def turn(k, before):
        at = count - 1 - k if reverse else k
        reached = at > here if reverse else at < here
        new = combine(before, jax.tree.map(lambda part: part[at], everything))
        return jax.tree.map(lambda a, b: jnp.where(reached, a, b), new, before)

    return lax.fori_loop(0, count, turn, start)


def features(points):
    feat_width = points.shape[-1]
    constant = jnp.ones(points.shape[:-1] + (1,), jnp.float32)
    products = (points[..., :, None] * points[..., None, :]).reshape(
        points.shape[:-1] + (feat_width * feat_width,)
    )
    return jnp.concatenate([constant, points * 0.5, products * quad_scale], axis=-1)


def feature_grad(grad_feat, points):
    feat_width = points.shape[-1]
    linear = grad_feat[..., 1 : 1 + feat_width] * 0.5
    square = grad_feat[..., 1 + feat_width :].reshape(points.shape[:-1] + (feat_width, feat_width))
    paired = square + jnp.swapaxes(square, -1, -2)
    return linear + quad_scale * jnp.sum(paired * points[..., None, :], axis=-1)


def segment_ids(doc_lengths, positions):
    starts = jnp.cumsum(doc_lengths, dtype=jnp.int32) - doc_lengths
    return jnp.sum((starts[None, :] <= positions[:, None]).astype(jnp.int32), axis=1) - 1


def carry_doc(earlier, latter):
    retained = 1.0 - latter[2]
    return (
        latter[0] + retained * earlier[0],
        latter[1] + retained * earlier[1],
        jnp.maximum(earlier[2], latter[2]),
    )


def on_device(query_key, values, out_grad, out_weight, doc_lengths):
    tokens = query_key.shape[0]
    head_count = out_weight.shape[0] // HEAD
    row_block = min(tokens, 512)
    offset = lax.axis_index("ctx") * tokens
    positions = offset + jnp.arange(tokens, dtype=jnp.int32)
    segment = segment_ids(doc_lengths, positions)
    open_before = segment_ids(doc_lengths, jnp.reshape(offset - 1, (1,)))[0]
    open_after = segment[tokens - 1]
    restart = (open_after != open_before).astype(jnp.float32)
    carried = (segment == open_before).astype(jnp.float32)
    ending = (segment == open_after).astype(jnp.float32)
    paired = query_key.reshape(tokens, head_count, 2, QK).transpose(1, 2, 0, 3)
    queries = paired[:, 0]
    keys_all = paired[:, 1]
    value_rows = values.reshape(tokens, head_count, HEAD).transpose(1, 0, 2)
    query_feat = features(queries.astype(jnp.float32)).astype(jnp.bfloat16)
    key_feat = features(keys_all.astype(jnp.float32)).astype(jnp.bfloat16)
    ending_feat = jnp.where(ending[None, :, None] > 0.5, key_feat, jnp.zeros_like(key_feat))
    state_local = jnp.einsum(
        "htf,htd->hfd", ending_feat, value_rows, preferred_element_type=jnp.float32
    )
    norm_local = jnp.sum(ending_feat.astype(jnp.float32), axis=1)
    identity = (jnp.zeros_like(state_local), jnp.zeros_like(norm_local), jnp.zeros((), jnp.float32))
    local_fwd = (state_local, norm_local, restart)
    incoming = prefix(local_fwd, "ctx", carry_doc, identity, False)
    state_b = incoming[0].astype(jnp.bfloat16)
    norm_in = incoming[1]
    full_out = lax.all_gather(out_grad, "head", axis=1, tiled=True)
    out_rows = lax.dot_general(
        full_out, out_weight, (((1,), (1,)), ((), ())), preferred_element_type=jnp.float32
    )
    grads_out = out_rows.reshape(tokens, head_count, HEAD).transpose(1, 0, 2)
    places = jnp.arange(tokens, dtype=jnp.int32)
    nadj_local = jnp.zeros_like(norm_local)
    row_span = slice(0, row_block)
    scores = (
        jnp.einsum("hid,hjd->hij", queries, keys_all, preferred_element_type=jnp.float32) * 0.25
    )
    visible = (places[None, :] <= places[row_span, None]) & (
        segment[row_span, None] == segment[None, :]
    )
    weight = jnp.where(visible[None], 1.0 + scores + 0.5 * scores * scores, 0.0)
    weight_b = weight.astype(jnp.bfloat16)
    from_state = jnp.einsum("hif,hfd->hid", query_feat, state_b, preferred_element_type=jnp.float32)
    numerator = (
        jnp.einsum("hij,hjd->hid", weight_b, value_rows, preferred_element_type=jnp.float32)
        + carried[None, :, None] * from_state
    )
    denominator = jnp.sum(weight, axis=2) + carried[None, :] * jnp.einsum(
        "hif,hf->hi", query_feat.astype(jnp.float32), norm_in, precision=highest
    )
    attended = numerator / denominator[:, :, None]
    attended_list = attended.astype(jnp.bfloat16)
    den_grad = -jnp.sum(grads_out * attended, axis=2) / denominator
    num_grad = (grads_out / denominator[:, :, None]).astype(jnp.bfloat16)
    mix_grad = (
        jnp.einsum("hid,hjd->hij", num_grad, value_rows, preferred_element_type=jnp.float32)
        + den_grad[:, :, None]
    )
    score_grad = jnp.where(visible[None], mix_grad * (1.0 + scores), 0.0).astype(jnp.bfloat16)
    value_grad = jnp.einsum("hij,hid->hjd", weight_b, num_grad, preferred_element_type=jnp.float32)
    key_grad = 0.25 * jnp.einsum(
        "hij,hid->hjd", score_grad, queries, preferred_element_type=jnp.float32
    )
    feat_grad = carried[None, :, None] * (
        jnp.einsum("hid,hfd->hif", num_grad, state_b, preferred_element_type=jnp.float32)
        + den_grad[:, :, None] * norm_in[:, None, :]
    )
    query_list = 0.25 * jnp.einsum(
        "hij,hjd->hid", score_grad, keys_all, preferred_element_type=jnp.float32
    ) + feature_grad(feat_grad, queries.astype(jnp.float32))
    near_feat = jnp.where(carried[None, :, None] > 0.5, query_feat, jnp.zeros_like(query_feat))
    adj_local = jnp.einsum("hif,hid->hfd", near_feat, num_grad, preferred_element_type=jnp.float32)
    nadj_local = nadj_local + jnp.einsum(
        "hif,hi->hf", near_feat.astype(jnp.float32), den_grad, precision=highest
    )
    attended_all = attended_list.transpose(1, 0, 2).reshape(tokens, head_count * HEAD)
    term = lax.dot_general(
        attended_all, full_out, (((0,), (0,)), ((), ())), preferred_element_type=jnp.float32
    )
    proj_grad = lax.psum_scatter(term, "ctx", scatter_dimension=1, tiled=True)
    local_back = (adj_local, nadj_local, restart)
    outgoing = prefix(local_back, "ctx", carry_doc, identity, True)
    adjoint_b = outgoing[0].astype(jnp.bfloat16)
    ending_col = ending[None, :, None]
    value_grad = value_grad + ending_col * jnp.einsum(
        "htf,hfd->htd", key_feat, adjoint_b, preferred_element_type=jnp.float32
    )
    key_feat_grad = ending_col * (
        jnp.einsum("htd,hfd->htf", value_rows, adjoint_b, preferred_element_type=jnp.float32)
        + outgoing[1][:, None, :]
    )
    key_grad = key_grad + feature_grad(key_feat_grad, keys_all.astype(jnp.float32))
    qk_grad = (
        jnp.stack([query_list, key_grad], axis=2)
        .transpose(1, 0, 2, 3)
        .reshape(tokens, head_count * 2 * QK)
        .astype(jnp.bfloat16)
    )
    value_out = (
        value_grad.transpose(1, 0, 2).reshape(tokens, head_count * HEAD).astype(jnp.bfloat16)
    )
    return (qk_grad, value_out, proj_grad)


def solution(mesh):
    placed = (P("ctx", "head"), P("ctx", "head"), P("ctx", "head"), P("head", None), P())
    return jax.shard_map(
        on_device,
        mesh=mesh,
        in_specs=placed,
        out_specs=(P("ctx", "head"), P("ctx", "head"), P("head", "ctx")),
        check_vma=False,
    )
```

profile of v0, /device:TPU:14, one launch (start us, length us, event | category | flops | bytes accessed | tf_op | source)
XLA Modules:
  0.0 458.2 jit_solution(9752410014046797347)
XLA Ops:
  17.4 50.7 %all-reduce = f32[32]{0:T(128)S(1)} all-reduce(f32[32]{0:T(128)S(1)} %dynamic-update-slice), channel_id=1, replica_groups=mesh['ctx'=32,'head'=8] {'ctx'}, use_global_device_ids=true, to_apply=%add | all-reduce | flops 32 | bytes 256
  68.8 36.0 %all-gather.4 = f32[32,4,273]{2,1,0:T(4,128)S(1)} all-gather(f32[1,4,273]{2,1,0:T(4,128)S(1)} %bitcast.170), channel_id=3, replica_groups=mesh['ctx'=32,'head'=8] {'ctx'}, dimensions={0}, use_global_device_ids=true | all-gather | bytes 144144 | tf_op jit(solution)/shard_map/all_gather | solution.py:18
  107.7 2.1 copy-done.15
  109.8 2.1 fusion.27
  111.9 7.2 %fusion.52 = f32[512,512]{0,1:T(8,128)} fusion(bf16[512,4096]{1,0:T(8,128)(2,1)} %all-gather.10.cloned.1.call-done, bf16[512,4096]{1,0:T(8,128)(2,1)} %param.12), kind=kOutput, calls=%fused_computation.95 | convolution fusion | flops 2147483648 | bytes 9437184 | tf_op jit(solution)/shard_map/dot_general | solution.py:92
  119.1 29.3 %all-gather.12.cloned.1.call-done = f32[128,273,128]{2,1,0:T(8,128)} async-done(((f32[4,273,128]{2,1,0:T(8,128)}), f32[128,273,128]{2,1,0:T(8,128)}) %all-gather.12.cloned.1.call-update) | async-done | bytes 17891344 | tf_op jit(solution)/shard_map/all_gather | solution.py:18
  148.4 91.4 %while.34 = (s32[]{:T(128)}, f32[4,273,128]{2,1,0:T(8,128)S(1)}, f32[4,273]{1,0:T(4,128)S(1)}, s32[]{:T(128)}, f32[32,4,273,128]{3,2,1,0:T(8,128)}, /*index=5*/f...) while((s32[]{:T(128)}, f32[4,273,128]{2,1,0:T(8,128)S(1)}, ...), condition=%wide.region_6.7_spmd.clone, body=%wide.region_5.6_spmd.clone.sunk | while | flops 563477 | bytes 1690579 | solution.py:29
  241.4 1.8 multiply_reduce_fusion
  247.6 1.7 slice.31
  249.3 25.8 %all-gather.5 = f32[32,4,273]{2,1,0:T(4,128)} all-gather(f32[1,4,273]{2,1,0:T(4,128)S(1)} %bitcast.171), channel_id=5, replica_groups=mesh['ctx'=32,'head'=8] {'ctx'}, dimensions={0}, use_global_device_ids=true | all-gather | bytes 144144 | tf_op jit(solution)/shard_map/all_gather | solution.py:18
  276.4 2.2 fusion.49
  278.7 5.7 %fusion.53 = f32[512,4096]{1,0:T(8,128)} fusion(bf16[512,512]{0,1:T(8,128)(2,1)S(1)} %bitcast.152, bf16[512,4096]{1,0:T(8,128)(2,1)S(1)} %copy-done.3), kind=kOutput, calls=%fused_computation.96 | convolution fusion | flops 2147483648 | bytes 13107200 | tf_op jit(solution)/shard_map/dot_general | solution.py:141
  284.4 41.4 %all-gather.14.cloned.1.call-done = f32[128,273,128]{2,1,0:T(8,128)} async-done(((f32[4,273,128]{2,1,0:T(8,128)}), f32[128,273,128]{2,1,0:T(8,128)}) %all-gather.14.cloned.1.call-update) | async-done | bytes 17891344 | tf_op jit(solution)/shard_map/all_gather | solution.py:18
  325.7 112.4 %while.35 = (s32[]{:T(128)}, f32[4,273,128]{2,1,0:T(8,128)S(1)}, f32[4,273]{1,0:T(4,128)S(1)}, s32[]{:T(128)}, f32[32,4,273,128]{3,2,1,0:T(8,128)}, /*index=5*/f...) while((s32[]{:T(128)}, f32[4,273,128]{2,1,0:T(8,128)S(1)}, ...), condition=%wide.region_10.11_spmd.clone, body=%wide.region_9.10_spmd.clone.sunk | while | flops 563481 | bytes 1690641 | solution.py:29
  341.0 1.6 fusion.74
  344.5 1.6 fusion.74
  348.0 1.6 fusion.74
  351.6 1.6 fusion.74
  355.1 1.6 fusion.74
  358.6 1.6 fusion.74
  362.2 1.6 fusion.74
  365.7 1.6 fusion.74
  369.2 1.6 fusion.74
  386.8 1.6 fusion.74
  390.3 1.6 fusion.74
  393.8 1.6 fusion.74
  397.3 1.6 fusion.74
  404.3 1.6 fusion.74
  421.9 1.6 fusion.74
  438.1 3.0 fusion.12
  441.1 2.0 copy.75
  445.3 3.6 fusion.7
  (265 shorter events, 162.3 us)
Async XLA Ops:
  7.2 6.8 %copy-start = (bf16[512,512]{1,0:T(8,128)(2,1)S(1)}, bf16[512,512]{1,0:T(8,128)(2,1)}, u32[]{:S(2)}) copy-start(bf16[512,512]{1,0:T(8,128)(2,1)} %param.10) | copy-start | bytes 1572868
  7.2 104.7 %all-gather.10.cloned.1.call-start = ((), (), s32[]{:S(2)}) async-start(), calls=%async_computation.1 | async-start | bytes 4718592 | tf_op jit(solution)/shard_map/all_gather | solution.py:91
  7.9 140.5 %all-gather.12.cloned.1.call-start = ((), (), s32[]{:S(2)}) async-start(), calls=%async_computation.3 | async-start | bytes 18923520 | tf_op jit(solution)/shard_map/all_gather | solution.py:18
  12.8 93.5 %copy-start.5 = (bf16[512,4,2,16]{0,3,1,2:T(8,128)(2,1)}, bf16[512,4,2,16]{0,3,1,2:T(8,128)(2,1)S(1)}, u32[]{:S(2)}) copy-start(bf16[512,4,2,16]{0,3,1,2:T(8,128)(2,1)S(1)} %copy.117) | copy-start | bytes 393220
  13.9 93.8 %copy-start.4 = (bf16[4,512,16,16]{1,3,2,0:T(8,128)(2,1)}, bf16[4,512,16,16]{1,3,2,0:T(8,128)(2,1)S(1)}, u32[]{:S(2)}) copy-start(bf16[4,512,16,16]{1,3,2,0:T(8,128)(2,1)S(1)} %multiply_convert_fusion) | copy-start | bytes 3145732
  13.9 2.2 copy-start.14
  15.4 310.4 %all-gather.14.cloned.1.call-start = ((), (), s32[]{:S(2)}) async-start(), calls=%async_computation.4 | async-start | bytes 18923520 | tf_op jit(solution)/shard_map/all_gather | solution.py:18
  105.0 2.7 copy-start.11
  107.7 2.1 copy-start.15
  148.4 91.4 %copy-start.7 = (bf16[4,512,16,16]{1,3,2,0:T(8,128)(2,1)S(1)}, bf16[4,512,16,16]{1,3,2,0:T(8,128)(2,1)}, u32[]{:S(2)}) copy-start(bf16[4,512,16,16]{1,3,2,0:T(8,128)(2,1)} %multiply_convert_fusion.1) | copy-start | bytes 3145732
  239.8 1.2 copy-start.13
  239.8 1.5 copy-start.17
  243.1 1.4 copy-start.9
  244.6 207.1 %reduce-scatter.2.cloned.1.call-start = ((), (), s32[]{:S(2)}) async-start(), calls=%async_computation.2 | async-start | bytes 8650752 | tf_op jit(solution)/shard_map/reduce_scatter | solution.py:144
  244.6 1.1 copy-start.10
  246.2 1.4 copy-start.1
  247.6 27.5 %copy-start.8 = (f32[4,512,128]{1,2,0:T(8,128)S(1)}, f32[4,512,128]{1,2,0:T(8,128)}, u32[]{:S(2)}) copy-start(f32[4,512,128]{1,2,0:T(8,128)} %get-tuple-element.413) | copy-start | bytes 3145732
  247.6 27.6 %copy-start.12 = (pred[512,512]{0,1:T(8,128)(4,1)S(1)}, pred[512,512]{0,1:T(8,128)(4,1)}, u32[]{:S(2)}) copy-start(pred[512,512]{0,1:T(8,128)(4,1)} %copy-done.11) | copy-start | bytes 786436
  247.6 27.6 %copy-start.16 = (f32[4,512,512]{1,2,0:T(8,128)S(1)}, f32[4,512,512]{1,2,0:T(8,128)}, u32[]{:S(2)}) copy-start(f32[4,512,512]{1,2,0:T(8,128)} %copy-done.15) | copy-start | bytes 12582916
  276.3 2.3 copy-start.3
  443.7 1.6 copy-start.2
  445.3 3.6 copy-start.6
Sparse Core Ops, SparseCore 0:
  9.8 57.6 all-gather.9
  70.0 78.3 all-gather.11
  244.7 81.0 all-gather.13
  330.2 99.7 reduce-scatter.1
where the time goes:
time: 466 us; the launch traced here: 458 us
  other arithmetic  131 us (28%)
  blocking collectives  113 us (24%)
  waiting for transfers between devices  71.4 us (15%)
  local copies, waits for them, and re-layouts  53.2 us (11%)
  loops' own time  42.4 us (9%)
  matrix products  32 us (7%)
  between operations  15.5 us (3%)
    select_n x128, other arithmetic, turn(): return jax.tree.map(lambda a, b: jnp.where(reached, a, b), new, before)  122 us
    all_gather x2, waiting for transfers between devices, prefix(): everything = jax.tree.map(lambda part: lax.all_gather(part, axis), x)  70.7 us
    all_gather x2, blocking collectives, prefix(): everything = jax.tree.map(lambda part: lax.all_gather(part, axis), x)  61.8 us
    unnamed x1, blocking collectives  50.7 us
    another operation x2, loops' own time, prefix(): return lax.fori_loop(0, count, turn, start)  42.4 us
    dynamic_slice x64, local copies, waits for them, and re-layouts, turn(): new = combine(before, jax.tree.map(lambda part: part[at], everything))  39.1 us
    unnamed x42, local copies, waits for them, and re-layouts  10.8 us
  transfers between devices with their start and end apart: 4, of which 2 were waited for; matrix products, arithmetic and copies ran while one was open for 30% of the time, Pallas kernels for 0%

commit v1 on v0

v1 whole, which is shorter than its diff:
```python
import functools
import math

import jax
import jax.numpy as jnp
import numpy as np
from jax import lax
from jax.experimental import pallas as pl
from jax.experimental.pallas import tpu as pltpu
from jax.sharding import PartitionSpec as P

HEAD = 128
QK = 16
HEADS = 4
TOK = 512
FEAT = 160
QUAD = 0.25 / math.sqrt(2.0)
bf16 = jnp.bfloat16
f32 = jnp.float32
LIMIT = 56 * 1024 * 1024


def feature_tables():
    pairs = [(a, b) for a in range(QK) for b in range(a, QK)]
    pick = np.zeros((FEAT, 2 * QK), np.float32)
    cols = np.zeros((FEAT, HEAD), np.float32)
    cols[0, :4] = (1.0, 1.0, 1.0, 1.0)
    for a in range(QK):
        pick[1 + a, a] = 1.0
        cols[1 + a, :4] = (0.0, 1.0, 0.5, 1.0)
    for n, (a, b) in enumerate(pairs):
        row = 1 + QK + n
        pick[row, a] = 1.0
        pick[row, QK + b] = 1.0
        cols[row, :4] = (0.0, 0.0, QUAD, 1.0 if a == b else 2.0)
    return pick, pick.T.copy(), cols


def shift(k):
    return [(i, i + k) for i in range(32) if 0 <= i + k < 32]


def dot(a, b, ca, cb):
    return lax.dot_general(a, b, (((ca,), (cb,)), ((), ())), preferred_element_type=f32)


def call(body, outs, n_in, flops, nbytes, scalar=True):
    specs = [pl.BlockSpec(memory_space=pltpu.VMEM)] * n_in
    if scalar:
        specs = [pl.BlockSpec(memory_space=pltpu.SMEM)] + specs
    return pl.pallas_call(
        body,
        out_shape=[jax.ShapeDtypeStruct(s, t) for s, t in outs],
        in_specs=specs,
        out_specs=[pl.BlockSpec(memory_space=pltpu.VMEM)] * len(outs),
        compiler_params=pltpu.CompilerParams(vmem_limit_bytes=LIMIT),
        cost_estimate=pl.CostEstimate(flops=flops, bytes_accessed=nbytes, transcendentals=0),
    )


def lifted(pick, cols, x):
    a = dot(pick[:, :QK], x, 1, 0) + cols[:, 0:1]
    b = dot(pick[:, QK : 2 * QK], x, 1, 0) + cols[:, 1:2]
    return a, b, ((a * b) * cols[:, 2:3]).astype(bf16)


def split(x):
    high = x.astype(bf16)
    return high, (x - high.astype(f32)).astype(bf16)


def chain(pick_t, cols, g, a, b):
    scaled = g * cols[:, 2:3]
    out = jnp.zeros((QK, TOK), f32)
    for table, other in ((pick_t[:QK], b), (pick_t[QK : 2 * QK], a)):
        high, low = split(scaled * other)
        out = out + dot(table, high, 1, 0) + dot(table, low, 1, 0)
    return out


def put_norms(ref, norms):
    lane = lax.broadcasted_iota(jnp.int32, (FEAT, HEAD), 1)
    total = jnp.zeros((FEAT, HEAD), f32)
    for h in range(HEADS):
        high, low = split(norms[h])
        total = jnp.where(lane == h, high.astype(f32), total)
        total = jnp.where(lane == HEADS + h, low.astype(f32), total)
    ref[HEADS] = total.astype(bf16)


def norm_of(near, far, keep, h):
    def one(ref):
        part = ref[HEADS].astype(f32)
        return part[:, h : h + 1] + part[:, HEADS + h : HEADS + h + 1]

    return one(near) + keep * one(far)


def state_of(near, far, keep, h):
    return (near[h].astype(f32) + keep * far[h].astype(f32)).astype(bf16)


def local_state(ids, lens, qk, v, pick, cols, out, qkt, aux):
    off = ids[0].astype(f32)
    length = lens[...].astype(f32)
    later = lax.broadcasted_iota(jnp.int32, (128, 128), 1) < lax.broadcasted_iota(
        jnp.int32, (128, 128), 0
    )
    first = jnp.sum(jnp.where(later, length, 0.0), axis=1, keepdims=True) - off

    def doc_at(where_to):
        return jnp.max(jnp.where(first <= where_to, first, -1e9), axis=0, keepdims=True)

    start = doc_at(lax.broadcasted_iota(jnp.int32, (128, TOK), 1).astype(f32))
    last, prev, far = doc_at(TOK - 1.0), doc_at(-1.0), doc_at(3 * TOK - 1.0)
    ending = (start == last).astype(f32)
    aux[0:1] = start
    aux[1:2] = ending
    aux[2:3] = (start < 0.0).astype(f32)
    aux[3:4] = jnp.broadcast_to((last < 0.0).astype(f32), (1, TOK))
    aux[4:5] = jnp.broadcast_to((prev < -2.0 * TOK).astype(f32), (1, TOK))
    aux[5:6] = jnp.broadcast_to((far < 1.0 * TOK).astype(f32), (1, TOK))
    aux[6:8] = jnp.zeros((2, TOK), f32)
    qkt[...] = qk[...].astype(f32).T.astype(bf16)
    norms = []
    table, column = pick[...], cols[...]
    for h in range(HEADS):
        feat = lifted(table, column, qkt[32 * h + QK : 32 * h + 2 * QK])[2]
        feat = jnp.where(ending > 0.5, feat.astype(f32), 0.0)
        norms.append(jnp.sum(feat, axis=1, keepdims=True) * column[:, 3:4])
        state = dot(feat.astype(bf16), v[:, HEAD * h : HEAD * (h + 1)], 1, 0)
        out[h] = (state * column[:, 3:4]).astype(bf16)
    put_norms(out, norms)


def pair_sum(own, got, aux, out):
    keep = aux[3:4, 0:1]
    for h in range(HEADS):
        out[h] = (own[h].astype(f32) + keep * got[h].astype(f32)).astype(bf16)
    put_norms(out, [norm_of(own, got, keep, h) for h in range(HEADS)])


def scores_of(qkt, aux, h):
    q, k = qkt[32 * h : 32 * h + QK], qkt[32 * h + QK : 32 * h + 2 * QK]
    scores = dot(k, q, 0, 0) * 0.25
    row = lax.broadcasted_iota(jnp.int32, (TOK, TOK), 0)
    col = lax.broadcasted_iota(jnp.int32, (TOK, TOK), 1)
    visible = (row >= aux[0:1].astype(jnp.int32)) & (row <= col)
    return scores, visible, jnp.where(visible, 1.0 + scores + 0.5 * scores * scores, 0.0)


def attend(qkt, v, aux, pick, cols, near, far, att, quotient, dens):
    keep = aux[4:5, 0:1]
    carried = aux[2:3]
    table, column = pick[...], cols[...]
    for h in range(HEADS):
        rows = slice(HEAD * h, HEAD * (h + 1))
        weight = scores_of(qkt, aux, h)[2]
        feat = lifted(table, column, qkt[32 * h : 32 * h + QK])[2]
        norm = norm_of(near, far, keep, h)
        den = jnp.sum(weight, axis=0, keepdims=True)
        den = den + carried * jnp.sum(feat.astype(f32) * norm, axis=0, keepdims=True)
        num = dot(v[:, rows], weight.astype(bf16), 0, 0)
        num = num + carried * dot(state_of(near, far, keep, h), feat, 0, 0)
        y = num / den
        quotient[rows] = y
        att[rows] = y.astype(bf16)
        dens[h : h + 1] = den
    dens[HEADS:] = jnp.ones((8 - HEADS, TOK), f32)


def shard_of(ids, k):
    return lax.rem(ids[3] + k + 8, 8)


def partial_terms(count, ids, att, *refs):
    parts, (send, keep) = refs[: 2 * count], refs[2 * count :]
    first = ids[2] == 0
    half = TOK // 2
    for n in range(count):
        both = dot(att[:, :half], parts[2 * n][...], 1, 0)
        both = (both + dot(att[:, half:], parts[2 * n + 1][...], 1, 0)).astype(bf16)
        for j in range(2):
            even = both[:, 256 * j : 256 * j + HEAD]
            odd = both[:, 256 * j + HEAD : 256 * (j + 1)]
            send[2 * n + j] = jnp.where(first, odd, even)
            keep[2 * n + j] = jnp.where(first, even, odd)


def sum_cores(steps, ids, *refs):
    count = len(steps)
    out = refs[2 * count]
    for group, shards in enumerate(steps):
        for n, k in enumerate(shards):
            for j in range(2):
                total = refs[group][2 * n + j].astype(f32) + refs[count + group][2 * n + j].astype(f32)
                out[2 * shard_of(ids, k) + j] = total.astype(bf16)


def upstream(order, ids, w, *refs):
    parts, up = refs[:-1], refs[-1]
    half = TOK // 2
    for p in range(2):
        total = jnp.zeros((TOK, half), f32)
        for n, k in enumerate(order):
            at = pl.multiple_of(shard_of(ids, k) * TOK, TOK)
            total = total + dot(w[:, pl.ds(at, TOK)], parts[2 * n + p][...], 1, 1)
        up[:, half * p : half * (p + 1)] = total


def local_adjoint(up, quotient, dens, qkt, aux, pick, cols, ng, dg, out):
    carried = aux[2:3]
    table, column = pick[...], cols[...]
    norms = []
    for h in range(HEADS):
        rows = slice(HEAD * h, HEAD * (h + 1))
        inv = 1.0 / dens[h : h + 1]
        upstream = up[rows]
        den_grad = -jnp.sum(upstream * quotient[rows], axis=0, keepdims=True) * inv
        num_grad = (upstream * inv).astype(bf16)
        ng[rows] = num_grad
        dg[h : h + 1] = den_grad
        feat = lifted(table, column, qkt[32 * h : 32 * h + QK])[2]
        feat = feat.astype(f32) * carried
        norms.append(jnp.sum(feat * den_grad, axis=1, keepdims=True) * column[:, 3:4])
        out[h] = (dot(feat.astype(bf16), num_grad, 1, 1) * column[:, 3:4]).astype(bf16)
    dg[HEADS:] = jnp.zeros((8 - HEADS, TOK), f32)
    put_norms(out, norms)


def local_grads(ng, dg, qkt, v, aux, pick, pick_t, cols, near, far, qkg, vg):
    keep = aux[4:5, 0:1]
    carried = aux[2:3]
    table, column = pick[...], cols[...]
    for h in range(HEADS):
        rows = slice(HEAD * h, HEAD * (h + 1))
        q, k = qkt[32 * h : 32 * h + QK], qkt[32 * h + QK : 32 * h + 2 * QK]
        scores, visible, weight = scores_of(qkt, aux, h)
        num_grad, den_grad = ng[rows], dg[h : h + 1]
        mix = dot(v[:, rows], num_grad, 1, 0) + den_grad
        score_grad = jnp.where(visible, mix * (1.0 + scores), 0.0).astype(bf16)
        vg[:, rows] = dot(weight.astype(bf16), num_grad, 1, 1)
        a, b, _ = lifted(table, column, q)
        g = dot(state_of(near, far, keep, h), num_grad, 1, 0)
        g = carried * (g + norm_of(near, far, keep, h) * den_grad)
        qkg[32 * h : 32 * h + QK] = 0.25 * dot(k, score_grad, 1, 0) + chain(
            pick_t[...], column, g, a, b
        )
        qkg[32 * h + QK : 32 * h + 2 * QK] = 0.25 * dot(q, score_grad, 1, 1)


def finish(qkg, vg, qkt, v, aux, pick, pick_t, cols, near, far, qk_out, v_out, acc):
    keep = aux[5:6, 0:1]
    ending = aux[1:2]
    table, column = pick[...], cols[...]
    for h in range(HEADS):
        rows = slice(HEAD * h, HEAD * (h + 1))
        a, b, feat = lifted(table, column, qkt[32 * h + QK : 32 * h + 2 * QK])
        feat = (feat.astype(f32) * ending).astype(bf16)
        adjoint = state_of(near, far, keep, h)
        v_out[:, rows] = (vg[:, rows] + dot(feat, adjoint, 0, 0)).astype(bf16)
        g = dot(adjoint, v[:, rows], 1, 1) + norm_of(near, far, keep, h)
        acc[32 * h : 32 * h + QK] = qkg[32 * h : 32 * h + QK]
        acc[32 * h + QK : 32 * h + 2 * QK] = qkg[32 * h + QK : 32 * h + 2 * QK] + chain(
            pick_t[...], column, g * ending, a, b
        )
    qk_out[...] = acc[...].T.astype(bf16)


def on_device(query_key, values, out_grad, out_weight, doc_lengths):
    c = lax.axis_index("ctx").astype(jnp.int32)
    ids = jnp.stack([c * TOK, c // 2, c % 2, lax.axis_index("head").astype(jnp.int32)])
    np_pick, np_pick_t, np_cols = feature_tables()
    pick, pick_t, cols = jnp.asarray(np_pick, bf16), jnp.asarray(np_pick_t, bf16), jnp.asarray(np_cols)
    slab = ((HEADS + 1, FEAT, HEAD), bf16)

    half = TOK // 2
    own = [out_grad[:half], out_grad[half:]]
    pieces = {0: own}
    ring = {d: [(i, (i + d) % 8) for i in range(8)] for d in (1, -1)}
    for step in range(1, 4):
        for d in (1, -1):
            before = pieces[-d * (step - 1)]
            pieces[-d * step] = [lax.ppermute(x, "head", ring[d]) for x in before]
    pieces[4] = [lax.ppermute(pieces[-3][0], "head", ring[1]), lax.ppermute(pieces[3][1], "head", ring[-1])]

    local, qkt, aux = call(
        local_state,
        [slab, ((128, TOK), bf16), ((8, TOK), f32)],
        5,
        2**27,
        2**21,
    )(ids, doc_lengths.reshape(1, 128), query_key, values, pick, cols)

    def exchange(mine, sign):
        got = lax.ppermute(mine, "ctx", shift(sign))
        pair = call(pair_sum, [slab], 3, 2**20, 2**20, False)(mine, got, aux)[0]
        return lax.ppermute(pair, "ctx", shift(sign)), lax.ppermute(pair, "ctx", shift(3 * sign))

    near, far = exchange(local, 1)
    att, quotient, dens = call(
        attend,
        [((TOK, TOK), bf16), ((TOK, TOK), f32), ((8, TOK), f32)],
        7,
        2**30,
        4 * 2**20,
        False,
    )(qkt, values, aux, pick, cols, near, far)

    steps = [(0, -1, 1), (-2, 2), (-3, 3), (4,)]
    keeps, gots = [], []
    for shards in steps:
        n = len(shards)
        block = ((2 * n, TOK, HEAD), bf16)
        send, keep = call(
            functools.partial(partial_terms, n), [block, block], 1 + 2 * n, n * 2**28, 2**20 * n
        )(ids, att, *[x for k in shards for x in pieces[k]])
        keeps.append(keep)
        gots.append(lax.ppermute(send, "ctx", [(i, i ^ 1) for i in range(32)]))
    summed = call(
        functools.partial(sum_cores, steps), [((16, TOK, HEAD), bf16)], 8, 2**21, 6 * 2**20
    )(ids, *keeps, *gots)[0]
    chips = [[2 * j + k for j in range(16)] for k in range(2)]
    spread = lax.all_to_all(summed, "ctx", 0, 0, axis_index_groups=chips)
    proj_grad = jnp.sum(spread.astype(f32), axis=0)

    order = [k for shards in steps for k in shards]
    up = call(functools.partial(upstream, order), [((TOK, TOK), f32)], 17, 2**32, 9 * 2**20)(
        ids, out_weight, *[x for k in order for x in pieces[k]]
    )[0]

    ng, dg, adj_local = call(
        local_adjoint,
        [((TOK, TOK), bf16), ((8, TOK), f32), slab],
        7,
        2**28,
        4 * 2**20,
        False,
    )(up, quotient, dens, qkt, aux, pick, cols)
    adj_near, adj_far = exchange(adj_local, -1)
    qkg, vg = call(
        local_grads, [((128, TOK), f32), ((TOK, TOK), f32)], 10, 2**31, 4 * 2**20, False
    )(ng, dg, qkt, values, aux, pick, pick_t, cols, near, far)
    qk_grad, value_grad = pl.pallas_call(
        finish,
        out_shape=[
            jax.ShapeDtypeStruct((TOK, 128), bf16),
            jax.ShapeDtypeStruct((TOK, TOK), bf16),
        ],
        in_specs=[pl.BlockSpec(memory_space=pltpu.VMEM)] * 10,
        out_specs=[pl.BlockSpec(memory_space=pltpu.VMEM)] * 2,
        scratch_shapes=[pltpu.VMEM((128, TOK), f32)],
        compiler_params=pltpu.CompilerParams(vmem_limit_bytes=LIMIT),
        cost_estimate=pl.CostEstimate(flops=2**29, bytes_accessed=4 * 2**20, transcendentals=0),
    )(qkg, vg, qkt, values, aux, pick, pick_t, cols, adj_near, adj_far)
    return (qk_grad, value_grad, proj_grad)


def solution(mesh):
    placed = (P("ctx", "head"), P("ctx", "head"), P("ctx", "head"), P("head", None), P())
    return jax.shard_map(
        on_device,
        mesh=mesh,
        in_specs=placed,
        out_specs=(P("ctx", "head"), P("ctx", "head"), P("head", "ctx")),
        check_vma=False,
    )
```

time: 466 us -> 134 us (0.29); the launches traced: 458 us -> 132 us
  other arithmetic: 131 us -> 1.62 us
  blocking collectives: 113 us -> 0 us
  starting transfers between devices: 0.16 us -> 52.1 us
  waiting for transfers between devices: 71.4 us -> 21.4 us
  Pallas kernels: 0 us -> 49.4 us
  local copies, waits for them, and re-layouts: 53.2 us -> 6.91 us
  loops' own time: 42.4 us -> 0 us
  matrix products: 32 us -> 0 us
  between operations: 15.5 us -> 0.98 us
    select_n x128 -> x0, other arithmetic: 122 us -> none  [turn(): return jax.tree.map(lambda a, b: jnp.where(reached, a, b), new, before)]
    all_gather x3 -> x0, waiting for transfers between devices: 70.7 us -> none  [the longest x2 70.7 us: prefix(): everything = jax.tree.map(lambda part: lax.all_gather(part, axis), x)]
    all_gather x2 -> x0, blocking collectives: 61.8 us -> none  [prefix(): everything = jax.tree.map(lambda part: lax.all_gather(part, axis), x)]
    unnamed x1 -> x0, blocking collectives: 50.7 us -> none
    pallas_call x0 -> x13, Pallas kernels: none -> 49.4 us  [the longest x4 12.3 us: on_device(): call(functools.partial(partial_terms, n), [block, block], 1 + 2 * n, n *...]
    ppermute x0 -> x24, starting transfers between devices: none -> 45.3 us  [the longest x12 22.4 us: on_device(): pieces[-d * step] = [lax.ppermute(x, 'head', ring[d]) for x in before]]
    another operation x2 -> x0, loops' own time: 42.4 us -> none  [prefix(): return lax.fori_loop(0, count, turn, start)]
    dynamic_slice x64 -> x0, local copies, waits for them, and re-layouts: 39.1 us -> none  [turn(): new = combine(before, jax.tree.map(lambda part: part[at], everything))]
  transfers between devices with their start and end apart: 4 -> 25, of which waited for: 2 -> 6; matrix products, arithmetic and copies ran while one was open for 30% -> 1% of each run, Pallas kernels for 0% -> 32%
where the time goes in v1:
time: 134 us; the launch traced here: 132 us
  starting transfers between devices  52.1 us (39%)
  Pallas kernels  49.4 us (37%)
  waiting for transfers between devices  21.4 us (16%)
  local copies, waits for them, and re-layouts  6.91 us (5%)
  other arithmetic  1.62 us (1%)
    ppermute x12, starting transfers between devices, on_device(): pieces[-d * step] = [lax.ppermute(x, 'head', ring[d]) for x in before]  22.4 us
    ppermute x2, waiting for transfers between devices, exchange(): got = lax.ppermute(mine, 'ctx', shift(sign))  13.1 us
    pallas_call x4, Pallas kernels, on_device(): call(functools.partial(partial_terms, n), [block, block], 1 + 2 * n, n *...  12.3 us
    ppermute x2, starting transfers between devices, exchange(): lax.ppermute(pair, 'ctx', shift(3 * sign))  10.7 us
    all_to_all x1, starting transfers between devices, on_device(): spread = lax.all_to_all(summed, 'ctx', 0, 0, axis_index_groups=chips)  6.75 us
    pallas_call x1, Pallas kernels, on_device(): call(functools.partial(upstream, order), [((TOK, TOK), f32)], 17, 2 ** 32...  6.64 us
    pallas_call x1, Pallas kernels, on_device(): call(local_grads, [((128, TOK), f32), ((TOK, TOK), f32)], 10, 2 ** 31, 4...  6.03 us
    unnamed x52, local copies, waits for them, and re-layouts  5.84 us
  transfers between devices with their start and end apart: 25, of which 6 were waited for; matrix products, arithmetic and copies ran while one was open for 1% of the time, Pallas kernels for 32%

profile of v1, /device:TPU:14, one launch (start us, length us, event | category | flops | bytes accessed | tf_op | source)
XLA Modules:
  0.0 132.4 jit_solution(6023836540488960399)
XLA Ops:
  1.3 3.1 %shard_map.104 = (bf16[5,160,128]{2,1,0:T(8,128)(2,1)}, bf16[128,512]{1,0:T(8,128)(2,1)}, f32[8,512]{1,0:T(8,128)}) custom-call(s32[4]{0:T(128)} %pad_add_fusion.ids, s32[1,128]{1,0:T(1,128)} %bitcast.5, bf16[512,128]{1,0:T(8,128)(2,1)} %qk.1, bf16[512,512]{1,0:T(8,128)(2,1)} %v.7, bf16[160,32]{1,0:T(8,128)(2,1)} %constant.43.clone.pick, ...), custom_call_target="tpu_custom_call" | custom-call | flops 134217728 | bytes 2097152 | tf_op jit(solution)/shard_map/pallas_call | solution.py:287
  4.4 1.9 %collective-permute-start.14 = (bf16[5,160,128]{2,1,0:T(8,128)(2,1)}, bf16[5,160,128]{2,1,0:T(8,128)(2,1)S(1)}, u32[]{:S(2)}, u32[]{:S(2)}) collective-permute-start(bf16[5,160,128]{2,1,0:T(8,128)(2,1)} %get-tuple-element.26.own), channel_id=1, source_target_pairs={{0,8},{8,16},{16,24},{24,32},{32,40},{40,48},{48,56},{56,64},{64,7... | collective-permute-start | bytes 614408 | tf_op jit(solution)/shard_map/ppermute | solution.py:296
  7.4 5.9 %collective-permute-start.3 = (bf16[256,512]{1,0:T(8,128)(2,1)S(1)}, bf16[256,512]{1,0:T(8,128)(2,1)S(1)}, u32[]{:S(2)}, u32[]{:S(2)}) collective-permute-start(bf16[256,512]{1,0:T(8,128)(2,1)S(1)} %get-tuple-element.45.refs_1_), channel_id=1, source_target_pairs={{0,7},{1,0},{2,1},{3,2},{4,3},{5,4},{6,5},{7,6},{8,15},{9,8},{10,9... | collective-permute-start | bytes 786440 | tf_op jit(solution)/shard_map/ppermute | solution.py:284
  13.3 3.2 %collective-permute-start.2 = (bf16[256,512]{1,0:T(8,128)(2,1)S(1)}, bf16[256,512]{1,0:T(8,128)(2,1)S(1)}, u32[]{:S(2)}, u32[]{:S(2)}) collective-permute-start(bf16[256,512]{1,0:T(8,128)(2,1)S(1)} %get-tuple-element.46.refs_0_), channel_id=1, source_target_pairs={{0,7},{1,0},{2,1},{3,2},{4,3},{5,4},{6,5},{7,6},{8,15},{9,8},{10,9... | collective-permute-start | bytes 786440 | tf_op jit(solution)/shard_map/ppermute | solution.py:284
  17.3 2.1 %shard_map.105 = bf16[5,160,128]{2,1,0:T(8,128)(2,1)} custom-call(bf16[5,160,128]{2,1,0:T(8,128)(2,1)} %get-tuple-element.26.own, bf16[5,160,128]{2,1,0:T(8,128)(2,1)} %copy-done.10, f32[8,512]{1,0:T(8,128)} %get-tuple-element.25.aux), custom_call_target="tpu_custom_call" | custom-call | flops 1048576 | bytes 1048576 | tf_op jit(solution)/shard_map/pallas_call | solution.py:297
  19.4 3.7 %collective-permute-start.16 = (bf16[5,160,128]{2,1,0:T(8,128)(2,1)}, bf16[5,160,128]{2,1,0:T(8,128)(2,1)S(1)}, u32[]{:S(2)}, u32[]{:S(2)}) collective-permute-start(bf16[5,160,128]{2,1,0:T(8,128)(2,1)} %shard_map.105), channel_id=1, source_target_pairs={{0,24},{8,32},{16,40},{24,48},{32,56},{40,64},{48,72},{56,80},{64,... | collective-permute-start | bytes 614408 | tf_op jit(solution)/shard_map/ppermute | solution.py:298
  23.1 2.6 %collective-permute-start.15 = (bf16[5,160,128]{2,1,0:T(8,128)(2,1)}, bf16[5,160,128]{2,1,0:T(8,128)(2,1)S(1)}, u32[]{:S(2)}, u32[]{:S(2)}) collective-permute-start(bf16[5,160,128]{2,1,0:T(8,128)(2,1)} %shard_map.105), channel_id=1, source_target_pairs={{0,8},{8,16},{16,24},{24,32},{32,40},{40,48},{48,56},{56,64},{64,7... | collective-permute-start | bytes 614408 | tf_op jit(solution)/shard_map/ppermute | solution.py:298
  25.7 3.3 %collective-permute-start.7 = (bf16[256,512]{1,0:T(8,128)(2,1)S(1)}, bf16[256,512]{1,0:T(8,128)(2,1)S(1)}, u32[]{:S(2)}, u32[]{:S(2)}) collective-permute-start(bf16[256,512]{1,0:T(8,128)(2,1)S(1)} %collective-permute-done.3.refs_5_), channel_id=1, source_target_pairs={{0,7},{1,0},{2,1},{3,2},{4,3},{5,4},{6,5},{7,6},{8,15},{9,8},{10,9... | collective-permute-start | bytes 786440 | tf_op jit(solution)/shard_map/ppermute | solution.py:284
  29.1 3.2 %collective-permute-start.6 = (bf16[256,512]{1,0:T(8,128)(2,1)S(1)}, bf16[256,512]{1,0:T(8,128)(2,1)S(1)}, u32[]{:S(2)}, u32[]{:S(2)}) collective-permute-start(bf16[256,512]{1,0:T(8,128)(2,1)S(1)} %collective-permute-done.2.refs_4_), channel_id=1, source_target_pairs={{0,7},{1,0},{2,1},{3,2},{4,3},{5,4},{6,5},{7,6},{8,15},{9,8},{10,9... | collective-permute-start | bytes 786440 | tf_op jit(solution)/shard_map/ppermute | solution.py:284
  33.1 5.0 %shard_map.106 = (bf16[512,512]{1,0:T(8,128)(2,1)}, f32[512,512]{1,0:T(8,128)}, f32[8,512]{1,0:T(8,128)}) custom-call(bf16[128,512]{1,0:T(8,128)(2,1)} %get-tuple-element.24.qkt, bf16[512,512]{1,0:T(8,128)(2,1)} %v.7, f32[8,512]{1,0:T(8,128)} %get-tuple-element.25.aux, bf16[160,32]{1,0:T(8,128)(2,1)} %constant.43.clone.pick, ...), custom_call_target="tpu_custom_call" | custom-call | flops 1073741824 | bytes 4194304 | tf_op jit(solution)/shard_map/pallas_call | solution.py:301
  38.1 3.3 %collective-permute-start.11 = (bf16[256,512]{1,0:T(8,128)(2,1)S(1)}, bf16[256,512]{1,0:T(8,128)(2,1)S(1)}, u32[]{:S(2)}, u32[]{:S(2)}) collective-permute-start(bf16[256,512]{1,0:T(8,128)(2,1)S(1)} %collective-permute-done.7.refs_9_.refs_3_), channel_id=1, source_target_pairs={{0,7},{1,0},{2,1},{3,2},{4,3},{5,4},{6,5},{7,6},{8,15},{9,8},{10,9... | collective-permute-start | bytes 786440 | tf_op jit(solution)/shard_map/ppermute | solution.py:284
  41.4 3.4 %collective-permute-start.10 = (bf16[256,512]{1,0:T(8,128)(2,1)S(1)}, bf16[256,512]{1,0:T(8,128)(2,1)S(1)}, u32[]{:S(2)}, u32[]{:S(2)}) collective-permute-start(bf16[256,512]{1,0:T(8,128)(2,1)S(1)} %collective-permute-done.6.refs_8_.refs_2_), channel_id=1, source_target_pairs={{0,7},{1,0},{2,1},{3,2},{4,3},{5,4},{6,5},{7,6},{8,15},{9,8},{10,9... | collective-permute-start | bytes 786440 | tf_op jit(solution)/shard_map/ppermute | solution.py:284
  44.8 3.8 %shard_map.111 = (bf16[6,512,128]{2,1,0:T(8,128)(2,1)}, bf16[6,512,128]{2,1,0:T(8,128)(2,1)}) custom-call(s32[4]{0:T(128)} %pad_add_fusion.ids, bf16[512,512]{1,0:T(8,128)(2,1)} %get-tuple-element.36.att, bf16[256,512]{1,0:T(8,128)(2,1)} %copy-done.5, bf16[256,512]{1,0:T(8,128)(2,1)} %copy-done.4, bf16[256,512]{1,0:T(8,128)(2,1)} %copy-done.15, ...), custom_call_target="tpu_custom_call" | custom-call | flops 805306368 | bytes 3145728 | tf_op jit(solution)/shard_map/pallas_call | solution.py:315
  48.6 3.0 %shard_map.112 = (bf16[4,512,128]{2,1,0:T(8,128)(2,1)}, bf16[4,512,128]{2,1,0:T(8,128)(2,1)}) custom-call(s32[4]{0:T(128)} %pad_add_fusion.ids, bf16[512,512]{1,0:T(8,128)(2,1)} %get-tuple-element.36.att, bf16[256,512]{1,0:T(8,128)(2,1)} %copy-done.19, bf16[256,512]{1,0:T(8,128)(2,1)} %copy-done.17, bf16[256,512]{1,0:T(8,128)(2,1)} %copy-done.18, ...), custom_call_target="tpu_custom_call" | custom-call | flops 536870912 | bytes 2097152 | tf_op jit(solution)/shard_map/pallas_call | solution.py:315
  52.3 3.1 %collective-permute-start.13 = (bf16[256,512]{1,0:T(8,128)(2,1)S(1)}, bf16[256,512]{1,0:T(8,128)(2,1)S(1)}, u32[]{:S(2)}, u32[]{:S(2)}) collective-permute-start(bf16[256,512]{1,0:T(8,128)(2,1)S(1)} %collective-permute-done.11.refs_13_.refs_3_), channel_id=1, source_target_pairs={{0,7},{1,0},{2,1},{3,2},{4,3},{5,4},{6,5},{7,6},{8,15},{9,8},{10,9... | collective-permute-start | bytes 786440 | tf_op jit(solution)/shard_map/ppermute | solution.py:285
  57.1 3.0 %shard_map.113 = (bf16[4,512,128]{2,1,0:T(8,128)(2,1)}, bf16[4,512,128]{2,1,0:T(8,128)(2,1)}) custom-call(s32[4]{0:T(128)} %pad_add_fusion.ids, bf16[512,512]{1,0:T(8,128)(2,1)} %get-tuple-element.36.att, bf16[256,512]{1,0:T(8,128)(2,1)} %copy-done.23, bf16[256,512]{1,0:T(8,128)(2,1)} %copy-done.21, bf16[256,512]{1,0:T(8,128)(2,1)} %copy-done.22, ...), custom_call_target="tpu_custom_call" | custom-call | flops 536870912 | bytes 2097152 | tf_op jit(solution)/shard_map/pallas_call | solution.py:315
  60.1 1.1 collective-permute-done.13.refs_15_.refs_1_
  61.2 3.4 %collective-permute-done.12.refs_14_.refs_0_ = bf16[256,512]{1,0:T(8,128)(2,1)S(1)} collective-permute-done((bf16[256,512]{1,0:T(8,128)(2,1)S(1)}, bf16[256,512]{1,0:T(8,128)(2,1)S(1)}, u32[]{:S(2)}, u32[]{:S(2)}) %collective-permute-start.12) | collective-permute-done | bytes 262176 | tf_op jit(solution)/shard_map/ppermute | solution.py:285
  65.4 2.4 %shard_map.114 = (bf16[2,512,128]{2,1,0:T(8,128)(2,1)}, bf16[2,512,128]{2,1,0:T(8,128)(2,1)}) custom-call(s32[4]{0:T(128)} %pad_add_fusion.ids, bf16[512,512]{1,0:T(8,128)(2,1)} %get-tuple-element.36.att, bf16[256,512]{1,0:T(8,128)(2,1)} %copy-done.7, bf16[256,512]{1,0:T(8,128)(2,1)} %copy-done.6), custom_call_target="tpu_custom_call" | custom-call | flops 268435456 | bytes 1048576 | tf_op jit(solution)/shard_map/pallas_call | solution.py:315
  67.9 1.7 %collective-permute-done.23.refs_7_ = bf16[2,512,128]{2,1,0:T(8,128)(2,1)S(1)} collective-permute-done((bf16[2,512,128]{2,1,0:T(8,128)(2,1)}, bf16[2,512,128]{2,1,0:T(8,128)(2,1)S(1)}, u32[]{:S(2)}, u32[]{:S(2)}) %collective-permute-start.23) | collective-permute-done | bytes 262176 | tf_op jit(solution)/shard_map/ppermute | solution.py:319
  70.4 4.0 %shard_map.115 = bf16[16,512,128]{2,1,0:T(8,128)(2,1)} custom-call(s32[4]{0:T(128)} %pad_add_fusion.ids, bf16[6,512,128]{2,1,0:T(8,128)(2,1)} %get-tuple-element.37.refs_0_, bf16[4,512,128]{2,1,0:T(8,128)(2,1)} %get-tuple-element.38.refs_1_, bf16[4,512,128]{2,1,0:T(8,128)(2,1)} %get-tuple-element.39.refs_2_, bf16[2,512,128]{2,1,0:T(8,128)(2,1)} %get-tuple-element.40.refs_3_, ...), custom_call_target="tpu_custom_call" | custom-call | flops 2097152 | bytes 6291456 | tf_op jit(solution)/shard_map/pallas_call | solution.py:320
  74.4 6.8 %all-to-all-start = ((bf16[16,512,128]{2,1,0:T(8,128)(2,1)}), bf16[16,512,128]{2,1,0:T(8,128)(2,1)S(1)}, u32[]{:S(2)}, u32[]{:S(2)}) async-start(bf16[16,512,128]{2,1,0:T(8,128)(2,1)} %shard_map.115), calls=%async_computation | async-start | bytes 4194304 | tf_op jit(solution)/shard_map/all_to_all | solution.py:324
  81.2 6.6 %shard_map.103.up = f32[512,512]{1,0:T(8,128)} custom-call(s32[4]{0:T(128)} %pad_add_fusion.ids, bf16[512,4096]{1,0:T(8,128)(2,1)} %w.1, bf16[256,512]{1,0:T(8,128)(2,1)} %copy-done.5, bf16[256,512]{1,0:T(8,128)(2,1)} %copy-done.4, bf16[256,512]{1,0:T(8,128)(2,1)} %copy-done.15, bf16[256,512]{1,0:T(8,128)(2,1)} %copy-done.13, bf16[256,512]{1,0:T(8,128)(2,1)} %copy-done.14, ...), custom_call_target="tpu_custom_call" | custom-call | flops 4294967296 | bytes 9437184 | tf_op jit(solution)/shard_map/pallas_call | solution.py:328
  87.8 3.4 %shard_map.107 = (bf16[512,512]{1,0:T(8,128)(2,1)}, f32[8,512]{1,0:T(8,128)}, bf16[5,160,128]{2,1,0:T(8,128)(2,1)}) custom-call(f32[512,512]{1,0:T(8,128)} %shard_map.103.up, f32[512,512]{1,0:T(8,128)} %get-tuple-element.27.quotient, f32[8,512]{1,0:T(8,128)} %get-tuple-element.28.dens, bf16[128,512]{1,0:T(8,128)(2,1)} %get-tuple-element.24.qkt, ...), custom_call_target="tpu_custom_call" | custom-call | flops 268435456 | bytes 4194304 | tf_op jit(solution)/shard_map/pallas_call | solution.py:332
  91.2 1.9 %collective-permute-start.17 = (bf16[5,160,128]{2,1,0:T(8,128)(2,1)}, bf16[5,160,128]{2,1,0:T(8,128)(2,1)S(1)}, u32[]{:S(2)}, u32[]{:S(2)}) collective-permute-start(bf16[5,160,128]{2,1,0:T(8,128)(2,1)} %get-tuple-element.33.own), channel_id=1, source_target_pairs={{8,0},{16,8},{24,16},{32,24},{40,32},{48,40},{56,48},{64,56},{72,6... | collective-permute-start | bytes 614408 | tf_op jit(solution)/shard_map/ppermute | solution.py:296
  93.1 13.1 %collective-permute-done.17.got = bf16[5,160,128]{2,1,0:T(8,128)(2,1)S(1)} collective-permute-done((bf16[5,160,128]{2,1,0:T(8,128)(2,1)}, bf16[5,160,128]{2,1,0:T(8,128)(2,1)S(1)}, u32[]{:S(2)}, u32[]{:S(2)}) %collective-permute-start.17) | collective-permute-done | bytes 204832 | tf_op jit(solution)/shard_map/ppermute | solution.py:296
  106.9 2.1 %shard_map.109 = bf16[5,160,128]{2,1,0:T(8,128)(2,1)} custom-call(bf16[5,160,128]{2,1,0:T(8,128)(2,1)} %get-tuple-element.33.own, bf16[5,160,128]{2,1,0:T(8,128)(2,1)} %copy-done.11, f32[8,512]{1,0:T(8,128)} %get-tuple-element.25.aux), custom_call_target="tpu_custom_call" | custom-call | flops 1048576 | bytes 1048576 | tf_op jit(solution)/shard_map/pallas_call | solution.py:297
  109.0 6.9 %collective-permute-start.19 = (bf16[5,160,128]{2,1,0:T(8,128)(2,1)}, bf16[5,160,128]{2,1,0:T(8,128)(2,1)S(1)}, u32[]{:S(2)}, u32[]{:S(2)}) collective-permute-start(bf16[5,160,128]{2,1,0:T(8,128)(2,1)} %shard_map.109), channel_id=1, source_target_pairs={{24,0},{32,8},{40,16},{48,24},{56,32},{64,40},{72,48},{80,56},{88,... | collective-permute-start | bytes 614408 | tf_op jit(solution)/shard_map/ppermute | solution.py:298
  115.9 2.1 %collective-permute-start.18 = (bf16[5,160,128]{2,1,0:T(8,128)(2,1)}, bf16[5,160,128]{2,1,0:T(8,128)(2,1)S(1)}, u32[]{:S(2)}, u32[]{:S(2)}) collective-permute-start(bf16[5,160,128]{2,1,0:T(8,128)(2,1)} %shard_map.109), channel_id=1, source_target_pairs={{8,0},{16,8},{24,16},{32,24},{40,32},{48,40},{56,48},{64,56},{72,6... | collective-permute-start | bytes 614408 | tf_op jit(solution)/shard_map/ppermute | solution.py:298
  118.0 6.0 %shard_map.108 = (f32[128,512]{1,0:T(8,128)}, f32[512,512]{1,0:T(8,128)}) custom-call(bf16[512,512]{1,0:T(8,128)(2,1)} %get-tuple-element.29.ng, f32[8,512]{1,0:T(8,128)} %get-tuple-element.30.dg, bf16[128,512]{1,0:T(8,128)(2,1)} %get-tuple-element.24.qkt, bf16[512,512]{1,0:T(8,128)(2,1)} %v.7, f32[8,512]{1,0:T(8,128)} %get-tuple-element.25.aux, ...), custom_call_target="tpu_custom_call" | custom-call | flops 2147483648 | bytes 4194304 | tf_op jit(solution)/shard_map/pallas_call | solution.py:341
  124.1 1.8 %collective-permute-done.19.far = bf16[5,160,128]{2,1,0:T(8,128)(2,1)S(1)} collective-permute-done((bf16[5,160,128]{2,1,0:T(8,128)(2,1)}, bf16[5,160,128]{2,1,0:T(8,128)(2,1)S(1)}, u32[]{:S(2)}, u32[]{:S(2)}) %collective-permute-start.19) | collective-permute-done | bytes 204832 | tf_op jit(solution)/shard_map/ppermute | solution.py:298
  126.6 4.8 %shard_map.110 = (bf16[512,128]{1,0:T(8,128)(2,1)}, bf16[512,512]{1,0:T(8,128)(2,1)}) custom-call(f32[128,512]{1,0:T(8,128)} %get-tuple-element.31.qkg, f32[512,512]{1,0:T(8,128)} %get-tuple-element.32.vg, bf16[128,512]{1,0:T(8,128)(2,1)} %get-tuple-element.24.qkt, bf16[512,512]{1,0:T(8,128)(2,1)} %v.7, f32[8,512]{1,0:T(8,128)} %get-tuple-element.25.aux, ...), custom_call_target="tpu_custom_call" | custom-call | flops 536870912 | bytes 4194304 | tf_op jit(solution)/shard_map/pallas_call | solution.py:344
  (86 shorter events, 9.5 us)
Async XLA Ops:
  4.4 12.2 %collective-permute-start.14 = (bf16[5,160,128]{2,1,0:T(8,128)(2,1)}, bf16[5,160,128]{2,1,0:T(8,128)(2,1)S(1)}, u32[]{:S(2)}, u32[]{:S(2)}) collective-permute-start(bf16[5,160,128]{2,1,0:T(8,128)(2,1)} %get-tuple-element.26.own), channel_id=1, source_target_pairs={{0,8},{8,16},{16,24},{24,32},{32,40},{40,48},{48,56},{56,64},{64,7... | collective-permute-start | bytes 614408 | tf_op jit(solution)/shard_map/ppermute | solution.py:296
  7.4 30.7 %copy-start.4 = (bf16[256,512]{1,0:T(8,128)(2,1)}, bf16[256,512]{1,0:T(8,128)(2,1)S(1)}, u32[]{:S(2)}) copy-start(bf16[256,512]{1,0:T(8,128)(2,1)S(1)} %get-tuple-element.45.refs_1_) | copy-start | bytes 786436
  7.4 30.7 %copy-start.5 = (bf16[256,512]{1,0:T(8,128)(2,1)}, bf16[256,512]{1,0:T(8,128)(2,1)S(1)}, u32[]{:S(2)}) copy-start(bf16[256,512]{1,0:T(8,128)(2,1)S(1)} %get-tuple-element.46.refs_0_) | copy-start | bytes 786436
  7.4 15.7 %collective-permute-start.3 = (bf16[256,512]{1,0:T(8,128)(2,1)S(1)}, bf16[256,512]{1,0:T(8,128)(2,1)S(1)}, u32[]{:S(2)}, u32[]{:S(2)}) collective-permute-start(bf16[256,512]{1,0:T(8,128)(2,1)S(1)} %get-tuple-element.45.refs_1_), channel_id=1, source_target_pairs={{0,7},{1,0},{2,1},{3,2},{4,3},{5,4},{6,5},{7,6},{8,15},{9,8},{10,9... | collective-permute-start | bytes 786440 | tf_op jit(solution)/shard_map/ppermute | solution.py:284
  13.3 12.4 %collective-permute-start.1 = (bf16[256,512]{1,0:T(8,128)(2,1)S(1)}, bf16[256,512]{1,0:T(8,128)(2,1)S(1)}, u32[]{:S(2)}, u32[]{:S(2)}) collective-permute-start(bf16[256,512]{1,0:T(8,128)(2,1)S(1)} %get-tuple-element.45.refs_1_), channel_id=1, source_target_pairs={{0,1},{1,2},{2,3},{3,4},{4,5},{5,6},{6,7},{7,0},{8,9},{9,10},{10,1... | collective-permute-start | bytes 786440 | tf_op jit(solution)/shard_map/ppermute | solution.py:284
  13.3 15.7 %collective-permute-start.2 = (bf16[256,512]{1,0:T(8,128)(2,1)S(1)}, bf16[256,512]{1,0:T(8,128)(2,1)S(1)}, u32[]{:S(2)}, u32[]{:S(2)}) collective-permute-start(bf16[256,512]{1,0:T(8,128)(2,1)S(1)} %get-tuple-element.46.refs_0_), channel_id=1, source_target_pairs={{0,7},{1,0},{2,1},{3,2},{4,3},{5,4},{6,5},{7,6},{8,15},{9,8},{10,9... | collective-permute-start | bytes 786440 | tf_op jit(solution)/shard_map/ppermute | solution.py:284
  16.6 12.5 %collective-permute-start = (bf16[256,512]{1,0:T(8,128)(2,1)S(1)}, bf16[256,512]{1,0:T(8,128)(2,1)S(1)}, u32[]{:S(2)}, u32[]{:S(2)}) collective-permute-start(bf16[256,512]{1,0:T(8,128)(2,1)S(1)} %get-tuple-element.46.refs_0_), channel_id=1, source_target_pairs={{0,1},{1,2},{2,3},{3,4},{4,5},{5,6},{6,7},{7,0},{8,9},{9,10},{10,1... | collective-permute-start | bytes 786440 | tf_op jit(solution)/shard_map/ppermute | solution.py:284
  19.4 13.0 %collective-permute-start.16 = (bf16[5,160,128]{2,1,0:T(8,128)(2,1)}, bf16[5,160,128]{2,1,0:T(8,128)(2,1)S(1)}, u32[]{:S(2)}, u32[]{:S(2)}) collective-permute-start(bf16[5,160,128]{2,1,0:T(8,128)(2,1)} %shard_map.105), channel_id=1, source_target_pairs={{0,24},{8,32},{16,40},{24,48},{32,56},{40,64},{48,72},{56,80},{64,... | collective-permute-start | bytes 614408 | tf_op jit(solution)/shard_map/ppermute | solution.py:298
  23.1 21.7 %copy-start.12 = (bf16[256,512]{1,0:T(8,128)(2,1)}, bf16[256,512]{1,0:T(8,128)(2,1)S(1)}, u32[]{:S(2)}) copy-start(bf16[256,512]{1,0:T(8,128)(2,1)S(1)} %collective-permute-done.3.refs_5_) | copy-start | bytes 786436
  23.1 9.2 %collective-permute-start.15 = (bf16[5,160,128]{2,1,0:T(8,128)(2,1)}, bf16[5,160,128]{2,1,0:T(8,128)(2,1)S(1)}, u32[]{:S(2)}, u32[]{:S(2)}) collective-permute-start(bf16[5,160,128]{2,1,0:T(8,128)(2,1)} %shard_map.105), channel_id=1, source_target_pairs={{0,8},{8,16},{16,24},{24,32},{32,40},{40,48},{48,56},{56,64},{64,7... | collective-permute-start | bytes 614408 | tf_op jit(solution)/shard_map/ppermute | solution.py:298
  25.7 19.1 %copy-start.13 = (bf16[256,512]{1,0:T(8,128)(2,1)}, bf16[256,512]{1,0:T(8,128)(2,1)S(1)}, u32[]{:S(2)}) copy-start(bf16[256,512]{1,0:T(8,128)(2,1)S(1)} %collective-permute-done.1.refs_3_) | copy-start | bytes 786436
  25.7 12.3 %collective-permute-start.7 = (bf16[256,512]{1,0:T(8,128)(2,1)S(1)}, bf16[256,512]{1,0:T(8,128)(2,1)S(1)}, u32[]{:S(2)}, u32[]{:S(2)}) collective-permute-start(bf16[256,512]{1,0:T(8,128)(2,1)S(1)} %collective-permute-done.3.refs_5_), channel_id=1, source_target_pairs={{0,7},{1,0},{2,1},{3,2},{4,3},{5,4},{6,5},{7,6},{8,15},{9,8},{10,9... | collective-permute-start | bytes 786440 | tf_op jit(solution)/shard_map/ppermute | solution.py:284
  29.1 15.7 %copy-start.14 = (bf16[256,512]{1,0:T(8,128)(2,1)}, bf16[256,512]{1,0:T(8,128)(2,1)S(1)}, u32[]{:S(2)}) copy-start(bf16[256,512]{1,0:T(8,128)(2,1)S(1)} %collective-permute-done.2.refs_4_) | copy-start | bytes 786436
  29.1 12.3 %collective-permute-start.5 = (bf16[256,512]{1,0:T(8,128)(2,1)S(1)}, bf16[256,512]{1,0:T(8,128)(2,1)S(1)}, u32[]{:S(2)}, u32[]{:S(2)}) collective-permute-start(bf16[256,512]{1,0:T(8,128)(2,1)S(1)} %collective-permute-done.1.refs_3_), channel_id=1, source_target_pairs={{0,1},{1,2},{2,3},{3,4},{4,5},{5,6},{6,7},{7,0},{8,9},{9,10},{10,1... | collective-permute-start | bytes 786440 | tf_op jit(solution)/shard_map/ppermute | solution.py:284
  29.1 15.7 %copy-start.15 = (bf16[256,512]{1,0:T(8,128)(2,1)}, bf16[256,512]{1,0:T(8,128)(2,1)S(1)}, u32[]{:S(2)}) copy-start(bf16[256,512]{1,0:T(8,128)(2,1)S(1)} %collective-permute-done.refs_2_) | copy-start | bytes 786436
  29.1 12.2 %collective-permute-start.6 = (bf16[256,512]{1,0:T(8,128)(2,1)S(1)}, bf16[256,512]{1,0:T(8,128)(2,1)S(1)}, u32[]{:S(2)}, u32[]{:S(2)}) collective-permute-start(bf16[256,512]{1,0:T(8,128)(2,1)S(1)} %collective-permute-done.2.refs_4_), channel_id=1, source_target_pairs={{0,7},{1,0},{2,1},{3,2},{4,3},{5,4},{6,5},{7,6},{8,15},{9,8},{10,9... | collective-permute-start | bytes 786440 | tf_op jit(solution)/shard_map/ppermute | solution.py:284
  32.3 12.4 %collective-permute-start.4 = (bf16[256,512]{1,0:T(8,128)(2,1)S(1)}, bf16[256,512]{1,0:T(8,128)(2,1)S(1)}, u32[]{:S(2)}, u32[]{:S(2)}) collective-permute-start(bf16[256,512]{1,0:T(8,128)(2,1)S(1)} %collective-permute-done.refs_2_), channel_id=1, source_target_pairs={{0,1},{1,2},{2,3},{3,4},{4,5},{5,6},{6,7},{7,0},{8,9},{9,10},{10,1... | collective-permute-start | bytes 786440 | tf_op jit(solution)/shard_map/ppermute | solution.py:284
  38.1 10.5 %copy-start.16 = (bf16[256,512]{1,0:T(8,128)(2,1)}, bf16[256,512]{1,0:T(8,128)(2,1)S(1)}, u32[]{:S(2)}) copy-start(bf16[256,512]{1,0:T(8,128)(2,1)S(1)} %collective-permute-done.7.refs_9_.refs_3_) | copy-start | bytes 786436
  38.1 13.6 %collective-permute-start.11 = (bf16[256,512]{1,0:T(8,128)(2,1)S(1)}, bf16[256,512]{1,0:T(8,128)(2,1)S(1)}, u32[]{:S(2)}, u32[]{:S(2)}) collective-permute-start(bf16[256,512]{1,0:T(8,128)(2,1)S(1)} %collective-permute-done.7.refs_9_.refs_3_), channel_id=1, source_target_pairs={{0,7},{1,0},{2,1},{3,2},{4,3},{5,4},{6,5},{7,6},{8,15},{9,8},{10,9... | collective-permute-start | bytes 786440 | tf_op jit(solution)/shard_map/ppermute | solution.py:284
  41.3 10.9 %collective-permute-start.9 = (bf16[256,512]{1,0:T(8,128)(2,1)S(1)}, bf16[256,512]{1,0:T(8,128)(2,1)S(1)}, u32[]{:S(2)}, u32[]{:S(2)}) collective-permute-start(bf16[256,512]{1,0:T(8,128)(2,1)S(1)} %collective-permute-done.5.refs_7_.refs_1_), channel_id=1, source_target_pairs={{0,1},{1,2},{2,3},{3,4},{4,5},{5,6},{6,7},{7,0},{8,9},{9,10},{10,1... | collective-permute-start | bytes 786440 | tf_op jit(solution)/shard_map/ppermute | solution.py:284
  41.4 14.4 %collective-permute-start.10 = (bf16[256,512]{1,0:T(8,128)(2,1)S(1)}, bf16[256,512]{1,0:T(8,128)(2,1)S(1)}, u32[]{:S(2)}, u32[]{:S(2)}) collective-permute-start(bf16[256,512]{1,0:T(8,128)(2,1)S(1)} %collective-permute-done.6.refs_8_.refs_2_), channel_id=1, source_target_pairs={{0,7},{1,0},{2,1},{3,2},{4,3},{5,4},{6,5},{7,6},{8,15},{9,8},{10,9... | collective-permute-start | bytes 786440 | tf_op jit(solution)/shard_map/ppermute | solution.py:284
  44.8 10.9 %collective-permute-start.8 = (bf16[256,512]{1,0:T(8,128)(2,1)S(1)}, bf16[256,512]{1,0:T(8,128)(2,1)S(1)}, u32[]{:S(2)}, u32[]{:S(2)}) collective-permute-start(bf16[256,512]{1,0:T(8,128)(2,1)S(1)} %collective-permute-done.4.refs_6_.refs_0_), channel_id=1, source_target_pairs={{0,1},{1,2},{2,3},{3,4},{4,5},{5,6},{6,7},{7,0},{8,9},{9,10},{10,1... | collective-permute-start | bytes 786440 | tf_op jit(solution)/shard_map/ppermute | solution.py:284
  48.6 19.3 %collective-permute-start.20 = (bf16[6,512,128]{2,1,0:T(8,128)(2,1)}, bf16[6,512,128]{2,1,0:T(8,128)(2,1)S(1)}, u32[]{:S(2)}, u32[]{:S(2)}) collective-permute-start(bf16[6,512,128]{2,1,0:T(8,128)(2,1)} %get-tuple-element.41), channel_id=1, source_target_pairs={{0,8},{8,0},{16,24},{24,16},{32,40},{40,32},{48,56},{56,48},{64,72... | collective-permute-start | bytes 2359304 | tf_op jit(solution)/shard_map/ppermute | solution.py:319
  51.7 16.1 %collective-permute-start.21 = (bf16[4,512,128]{2,1,0:T(8,128)(2,1)}, bf16[4,512,128]{2,1,0:T(8,128)(2,1)S(1)}, u32[]{:S(2)}, u32[]{:S(2)}) collective-permute-start(bf16[4,512,128]{2,1,0:T(8,128)(2,1)} %get-tuple-element.42), channel_id=1, source_target_pairs={{0,8},{8,0},{16,24},{24,16},{32,40},{40,32},{48,56},{56,48},{64,72... | collective-permute-start | bytes 1572872 | tf_op jit(solution)/shard_map/ppermute | solution.py:319
  52.3 9.0 %collective-permute-start.13 = (bf16[256,512]{1,0:T(8,128)(2,1)S(1)}, bf16[256,512]{1,0:T(8,128)(2,1)S(1)}, u32[]{:S(2)}, u32[]{:S(2)}) collective-permute-start(bf16[256,512]{1,0:T(8,128)(2,1)S(1)} %collective-permute-done.11.refs_13_.refs_3_), channel_id=1, source_target_pairs={{0,7},{1,0},{2,1},{3,2},{4,3},{5,4},{6,5},{7,6},{8,15},{9,8},{10,9... | collective-permute-start | bytes 786440 | tf_op jit(solution)/shard_map/ppermute | solution.py:285
  55.7 8.9 %collective-permute-start.12 = (bf16[256,512]{1,0:T(8,128)(2,1)S(1)}, bf16[256,512]{1,0:T(8,128)(2,1)S(1)}, u32[]{:S(2)}, u32[]{:S(2)}) collective-permute-start(bf16[256,512]{1,0:T(8,128)(2,1)S(1)} %collective-permute-done.8.refs_10_.refs_0_), channel_id=1, source_target_pairs={{0,1},{1,2},{2,3},{3,4},{4,5},{5,6},{6,7},{7,0},{8,9},{9,10},{10,1... | collective-permute-start | bytes 786440 | tf_op jit(solution)/shard_map/ppermute | solution.py:285
  60.1 9.4 %collective-permute-start.22 = (bf16[4,512,128]{2,1,0:T(8,128)(2,1)}, bf16[4,512,128]{2,1,0:T(8,128)(2,1)S(1)}, u32[]{:S(2)}, u32[]{:S(2)}) collective-permute-start(bf16[4,512,128]{2,1,0:T(8,128)(2,1)} %get-tuple-element.43), channel_id=1, source_target_pairs={{0,8},{8,0},{16,24},{24,16},{32,40},{40,32},{48,56},{56,48},{64,72... | collective-permute-start | bytes 1572872 | tf_op jit(solution)/shard_map/ppermute | solution.py:319
  67.8 1.7 %collective-permute-start.23 = (bf16[2,512,128]{2,1,0:T(8,128)(2,1)}, bf16[2,512,128]{2,1,0:T(8,128)(2,1)S(1)}, u32[]{:S(2)}, u32[]{:S(2)}) collective-permute-start(bf16[2,512,128]{2,1,0:T(8,128)(2,1)} %get-tuple-element.44), channel_id=1, source_target_pairs={{0,8},{8,0},{16,24},{24,16},{32,40},{40,32},{48,56},{56,48},{64,72... | collective-permute-start | bytes 786440 | tf_op jit(solution)/shard_map/ppermute | solution.py:319
  74.4 57.0 %all-to-all-start = ((bf16[16,512,128]{2,1,0:T(8,128)(2,1)}), bf16[16,512,128]{2,1,0:T(8,128)(2,1)S(1)}, u32[]{:S(2)}, u32[]{:S(2)}) async-start(bf16[16,512,128]{2,1,0:T(8,128)(2,1)} %shard_map.115), calls=%async_computation | async-start | bytes 4194304 | tf_op jit(solution)/shard_map/all_to_all | solution.py:324
  91.2 15.0 %collective-permute-start.17 = (bf16[5,160,128]{2,1,0:T(8,128)(2,1)}, bf16[5,160,128]{2,1,0:T(8,128)(2,1)S(1)}, u32[]{:S(2)}, u32[]{:S(2)}) collective-permute-start(bf16[5,160,128]{2,1,0:T(8,128)(2,1)} %get-tuple-element.33.own), channel_id=1, source_target_pairs={{8,0},{16,8},{24,16},{32,24},{40,32},{48,40},{56,48},{64,56},{72,6... | collective-permute-start | bytes 614408 | tf_op jit(solution)/shard_map/ppermute | solution.py:296
  109.0 16.9 %collective-permute-start.19 = (bf16[5,160,128]{2,1,0:T(8,128)(2,1)}, bf16[5,160,128]{2,1,0:T(8,128)(2,1)S(1)}, u32[]{:S(2)}, u32[]{:S(2)}) collective-permute-start(bf16[5,160,128]{2,1,0:T(8,128)(2,1)} %shard_map.109), channel_id=1, source_target_pairs={{24,0},{32,8},{40,16},{48,24},{56,32},{64,40},{72,48},{80,56},{88,... | collective-permute-start | bytes 614408 | tf_op jit(solution)/shard_map/ppermute | solution.py:298
  115.9 10.0 %collective-permute-start.18 = (bf16[5,160,128]{2,1,0:T(8,128)(2,1)}, bf16[5,160,128]{2,1,0:T(8,128)(2,1)S(1)}, u32[]{:S(2)}, u32[]{:S(2)}) collective-permute-start(bf16[5,160,128]{2,1,0:T(8,128)(2,1)} %shard_map.109), channel_id=1, source_target_pairs={{8,0},{16,8},{24,16},{32,24},{40,32},{48,40},{56,48},{64,56},{72,6... | collective-permute-start | bytes 614408 | tf_op jit(solution)/shard_map/ppermute | solution.py:298
  (19 other events, 40.7 us)
